TPU v7x, 128 devices: a whole 4x4x4 slice. The times are simulated.
128 devices in a mesh: dp: 32 (over x, y, z_lo), tensor: 4 (over z_hi, core).
Axes of the slice: x: 4, y: 4, z: 4 (z_hi: 2, z_lo: 2; z = z_hi * 2 + z_lo), core: 2. Of those that a mesh axis runs over, the one named last changes fastest.
Arguments:
- hidden: bfloat16 [32768, 1536], P(('dp', 'tensor')), may hold values from -6 to 6
- in_gain: float32 [1536], replicated, may hold values from 0.5 to 1.5
- proj_main: bfloat16 [1536, 2, 3072], P('dp', None, 'tensor'), may hold values from -0.15625 to 0.15625
- proj_step: bfloat16 [1536, 48], P('dp', 'tensor'), may hold values from -0.15625 to 0.15625
- proj_state: bfloat16 [1536, 256], P('dp'), may hold values from -0.15625 to 0.15625
- conv_inner: float32 [4, 3072], P(None, 'tensor'), may hold values from -3 to 3
- conv_inner_bias: float32 [3072], P('tensor'), may hold values from -0.5 to 0.5
- conv_state: float32 [4, 256], replicated, may hold values from -3 to 3
- conv_state_bias: float32 [256], replicated, may hold values from -0.5 to 0.5
- step_bias: float32 [48], P('tensor'), may hold values from -3 to -1
- decay_log: float32 [48], P('tensor'), may hold values from -4 to 1
- skip_gain: float32 [48], P('tensor'), may hold values from 0.5 to 1.5
- out_gain: float32 [3072], P('tensor'), may hold values from 0.5 to 1.5
- proj_out: bfloat16 [1536, 3072], P('dp', 'tensor'), may hold values from -0.109375 to 0.109375
- grad_out: bfloat16 [32768, 1536], P(('dp', 'tensor')), may hold values from -6 to 6
Outputs:
- new_hidden: bfloat16 [32768, 1536], P(('dp', 'tensor'))
- grad_hidden: bfloat16 [32768, 1536], P(('dp', 'tensor'))
- grad_in_gain: float32 [1536], replicated
- grad_proj_main: float32 [1536, 2, 3072], P('dp', None, 'tensor')
- grad_proj_step: float32 [1536, 48], P('dp', 'tensor')
- grad_proj_state: float32 [1536, 256], P('dp')
- grad_conv_inner: float32 [4, 3072], P(None, 'tensor')
- grad_conv_inner_bias: float32 [3072], P('tensor')
- grad_conv_state: float32 [4, 256], replicated
- grad_conv_state_bias: float32 [256], replicated
- grad_step_bias: float32 [48], P('tensor')
- grad_decay_log: float32 [48], P('tensor')
- grad_skip_gain: float32 [48], P('tensor')
- grad_out_gain: float32 [3072], P('tensor')
- grad_proj_out: float32 [1536, 3072], P('dp', 'tensor')
All inputs are finite; a program needn't handle non-finite values.
Results may differ from a plain program's by a relative error of at most 0.03.
Values may be sent and summed in bfloat16 or wider, within the bound.
A program may use at most 192 MiB of HBM per device.

v0:
```python
import functools

import jax
import jax.numpy as jnp
from jax import lax
from jax.experimental import pallas as pl
from jax.experimental.pallas import tpu as pltpu
from jax.sharding import PartitionSpec as P

MESH = pl.DeviceIdType.MESH
F32, BF16 = jnp.float32, jnp.bfloat16
EPS = 1e-5
T, SPAN, HEAD, GROUP = 512, 256, 64, 4
WIDE = GROUP * HEAD
INNER = 3072
COLS = 2560
STAGED = ((0, 256), (256, 768), (1024, 768), (1792, 768))
ORDERS = ("xyz", "yzx", "zxy")
RCHUNKS = ((0, 768), (768, 768), (1536, 512), (2048, 256), (2304, 128))
STATE_COL, INNER_COL = 2304, 1536
RCOLS = 2432
SUMS = 64


def sds(shape, dtype=F32):
    return jax.ShapeDtypeStruct(shape, dtype)


def place():
    dp, tp = lax.axis_index("dp"), lax.axis_index("tensor")
    return dict(x=dp // 8, y=(dp // 2) % 4, z=(tp // 2) * 2 + dp % 2, core=tp % 2)


def device_at(at):
    return ((at["x"] * 4 + at["y"]) * 2 + at["z"] % 2, (at["z"] // 2) * 2 + at["core"])


def moved(at, axis, by):
    return {**at, axis: (at[axis] + by) % 4}


def units(at, whole):
    return (slice(None) if "z" in whole else at["z"] // 2, slice(None) if "x" in whole else at["x"],
            slice(None) if "y" in whole else at["y"], slice(None) if "z" in whole else at["z"] % 2)


def greet(others):
    barrier = pltpu.get_barrier_semaphore()
    for other in others:
        pl.semaphore_signal(barrier, inc=1, device_id=device_at(other), device_id_type=MESH)
    return lambda: pl.semaphore_wait(barrier, len(others))


def half_of(ref, stage, piece, width, half):
    if stage == 0:
        return ref.at[pl.ds(2 * half, 2)] if piece == 0 else ref.at[:, pl.ds(2 * half, 2)]
    if stage == 1:
        return ref.at[pl.ds(2 * half, 2)] if piece < 2 else ref.at[half]
    return ref.at[:, pl.ds(half * (width // 2), width // 2)]


def half_shape(stage, piece, width):
    if stage == 0:
        return (2, 4, 16, width) if piece == 0 else (2, 2, 2, 16, width)
    return (2, 16, width)


def region_shape(stage, piece, width):
    whole = ORDERS[piece][:2 - stage]
    dims = ([2] if "z" in whole else []) + ([4] if "x" in whole else []) + ([4] if "y" in whole else []) + ([2] if "z" in whole else [])
    return tuple(dims) + (16, width)


def dot(a, b, ca=1, cb=0):
    return lax.dot_general(a, b, (((ca,), (cb,)), ((), ())), preferred_element_type=F32)


def lanes(rows, width=T):
    return lax.broadcasted_iota(jnp.int32, (rows, width), 1)


def later(u, k):
    return jnp.where(lanes(u.shape[0]) >= k, pltpu.roll(u, k, 1), 0.0) if k else u


def sooner(u, k):
    return jnp.where(lanes(u.shape[0]) < T - k, pltpu.roll(u, T - k, 1), 0.0) if k else u


def sig(v):
    return 1.0 / (1.0 + jnp.exp(-v))


def split(v):
    a = v.astype(BF16)
    r = v - a.astype(F32)
    b = r.astype(BF16)
    return a, b, (r - b.astype(F32)).astype(BF16)


def exact_dot(v, ones):
    n = v.shape[0]
    s = dot(jnp.concatenate(split(v), axis=0), ones)
    return s[:n] + s[n:2 * n] + s[2 * n:]


def tri(n, keep):
    r = lax.broadcasted_iota(jnp.int32, (n, n), 0)
    c = lax.broadcasted_iota(jnp.int32, (n, n), 1)
    return jnp.where(keep(r, c), 1.0, 0.0).astype(BF16)


def conv(u, cols):
    shifted = [later(u, k) for k in range(4)]
    p = cols[:, 4:5] + cols[:, 0:1] * shifted[0]
    for k in range(1, 4):
        p = p + cols[:, k:k + 1] * shifted[k]
    return p, shifted


def conv_back(dp, cols):
    du = cols[:, 0:1] * dp
    for k in range(1, 4):
        du = du + cols[:, k:k + 1] * sooner(dp, k)
    return du


def decay(cum_row, cum_col, b):
    return jnp.exp(jnp.minimum(cum_row[:, b * SPAN:(b + 1) * SPAN] - cum_col, 0.0))


def group_at(n):
    zh, c = n % 2, n // 2
    return zh, c, pl.multiple_of((zh * 3 + c) * WIDE, WIDE), zh * 16 + c * GROUP


def group_cols(prm, zh, c):
    return prm[zh, :, pl.ds(pl.multiple_of(c * WIDE, WIDE), WIDE)].T


def group_skip(prm, zh, c):
    cols = prm[zh, :, 0:128].T
    return pltpu.roll(jnp.broadcast_to(cols[:, 8:9], (128, 128)), 128 - c * GROUP, 0)


def forward_kernel(main_h, step_h, state_h, out_h, hidden_h, cot_h, cinner_h, cstate_h, offset_h, gain_h, state_offset_h, in_gain_h, bias_h, log_h, skip_h,
                   xt_o, zt_o, ut_o, dgt_o, vt_o, xst_o, dsil_o, gat_o, yt_o, w_o, wst_o, pa_o,
                   *rest):
    small_o, (step_w, hidden, cinner, cstate, offset, gain, state_offset, in_gain, bias, log, skip_gain, w, x, g, xt, gt, zt, ut, dgt, vt, xst, dsil, gat, yt, pa, acc, acc_in,
              sums, dtt, cumt, cumc, stept, statet, bc, bct, cbt, prm, spar,
              send, recv, local, w_sem, out_sem, swap_send, swap_recv) = rest[:11], rest[11:]
    at = place()
    z_hi = at["z"] // 2
    mate = {**at, "core": 1 - at["core"]}
    far = moved(at, "z", 2)
    entered = greet([moved(at, axis, by) for axis in "xyz" for by in (1, 3)] + [mate, far])
    mine = pl.ds(pl.multiple_of(at["core"] * 256, 256), 256)
    own_unit = w.at[units(at, "")]
    moves = [(step_h, step_w), (hidden_h, hidden), (cot_h, g.at[mine]), (cinner_h, cinner), (cstate_h, cstate), (offset_h, offset), (gain_h, gain),
             (state_offset_h, state_offset), (in_gain_h, in_gain), (bias_h, bias), (log_h, log), (skip_h, skip_gain)]
    params = len(moves)
    for piece in range(3):
        rows = pl.ds(piece * 16, 16)
        for source, begin, width in ((state_h.at[rows, pl.ds(pl.multiple_of(z_hi * 128, 128), 128)], 0, 128), (main_h.at[rows, pl.ds(768, 768)], 256, 768),
                                     (main_h.at[rows, pl.ds(0, 768)], 1024, 768), (out_h.at[rows], 1792, 768)):
            moves.append((source, own_unit.at[piece, :, pl.ds(begin, width)]))
    moves = [pltpu.make_async_copy(a, b, local.at[i]) for i, (a, b) in enumerate(moves)]
    for c in moves:
        c.start()
    moves[0].wait()
    step_rows = jnp.concatenate([step_w[...].astype(F32), jnp.zeros((116, 48), F32)], axis=0).T.astype(BF16)
    for piece in range(3):
        w[units(at, "") + (piece, slice(None), pl.ds(128, 128))] = step_rows[piece * 16:(piece + 1) * 16]
    for c in moves[params:]:
        c.wait()
    entered()

    def part(where, piece, stage, chunk):
        begin, width = STAGED[chunk] if stage == 2 else (0, COLS)
        return w.at[units(where, ORDERS[piece][:stage]) + (piece, slice(None), pl.ds(begin, width))]

    def flight(piece, stage, chunk, kind):
        axis, by = ORDERS[piece][stage], (1, 3)[kind % 2]
        width = STAGED[chunk][1] if stage == 2 else COLS
        if kind < 2:
            target = source = part(at, piece, stage, chunk)
        else:
            target = source = half_of(part(moved(at, axis, -by), piece, stage, chunk), 2 - stage, piece, width, kind - 2)
        sem = (stage + chunk if stage == 2 else stage, piece, kind)
        return pltpu.make_async_remote_copy(src_ref=source, dst_ref=target, send_sem=send.at[sem], recv_sem=recv.at[sem],
                                            device_id=device_at(moved(at, axis, by)), device_id_type=MESH)

    def fulls(stage, chunk=0):
        for piece in range(3):
            if stage > 0 and chunk == 0:
                for kind in (2, 3):
                    flight(piece, stage - 1, 0, kind).wait_recv()
            for kind in (0, 1):
                flight(piece, stage, chunk, kind).start()

    def halves(stage, chunk=0):
        for piece in range(3):
            for kind in (0, 1):
                flight(piece, stage, chunk, kind).wait_recv()
                flight(piece, stage, chunk, kind + 2).start()

    def arrived(chunk):
        for piece in range(3):
            for kind in (2, 3):
                flight(piece, 2, chunk, kind).wait_recv()

    fulls(0)
    for c in moves[1:params]:
        c.wait()

    prm[z_hi] = jnp.zeros((16, 768), F32)
    prm[z_hi, 0:4, :] = cinner[...]
    prm[z_hi, 4:5, :] = offset[...].reshape(1, 768)
    prm[z_hi, 5:6, :] = gain[...].reshape(1, 768)
    for i, ref in enumerate((bias, log, skip_gain)):
        prm[z_hi, 6 + i:7 + i, 0:12] = ref[...].reshape(1, 12)
    h = hidden[...].astype(F32)
    scale = lax.rsqrt(jnp.mean(h * h, axis=1, keepdims=True) + EPS)
    x[mine, :] = (h * scale * in_gain[...].reshape(1, 1536)).astype(BF16)
    swaps = [pltpu.make_async_remote_copy(src_ref=s, dst_ref=s, send_sem=swap_send.at[i], recv_sem=swap_recv.at[i],
                                          device_id=device_at(to), device_id_type=MESH)
             for i, (s, to) in enumerate([(x.at[mine], mate), (g.at[mine], mate), (prm.at[z_hi], far)])]
    for c in swaps:
        c.start()
    spar[...] = jnp.concatenate([cstate[...], state_offset[...].reshape(1, 256), jnp.zeros((11, 256), F32)], axis=0).T

    halves(0)
    fulls(1)
    out_copies = []

    def put(i, source, target):
        c = pltpu.make_async_copy(source, target, out_sem.at[i])
        c.start()
        out_copies.append(c)

    for c in swaps[:2]:
        c.wait_recv()
    xt[...] = x[...].T
    gt[...] = g[...].T
    put(0, xt, xt_o)
    halves(1)
    swaps[2].wait_recv()
    acc[...] = jnp.zeros_like(acc)
    sums[...] = jnp.zeros_like(sums)
    cumc[...] = jnp.zeros_like(cumc)
    fulls(2, 0)
    fulls(2, 1)
    halves(2, 0)
    halves(2, 1)
    fulls(2, 2)
    arrived(0)
    put(2, w.at[:, :, :, :, :, :, pl.ds(0, 256)], wst_o)

    def weight(zh, begin):
        return w[zh, :, :, :, :, :, pl.ds(begin, WIDE)].reshape(1536, WIDE)

    for zh in range(2):
        raw = dot(x[...], weight(zh, 0)).T.astype(BF16)
        statet[zh * 128:(zh + 1) * 128, :] = raw[:128]
        stept[zh * 16:(zh + 1) * 16, :] = raw[128:144]
    for q in range(4):
        r = slice(q * 64, (q + 1) * 64)
        p, _ = conv(statet[r, :].astype(F32), spar[r])
        bct[r, :] = (p * sig(p)).astype(BF16)
    bc[...] = bct[...].T
    upper = tri(SPAN, lambda r, c: r <= c)
    for b in range(2):
        rows = pl.ds(b * SPAN, SPAN)
        cbt[b] = dot(bc[rows, 0:128], bc[rows, 128:256], 1, 1) * upper.astype(F32)
    for zh in range(2):
        cols = prm[zh, :, 0:128].T
        v = stept[zh * 16:(zh + 1) * 16, :].astype(F32) + cols[:16, 6:7]
        dt = jnp.maximum(v, 0.0) + jnp.log1p(jnp.exp(-jnp.abs(v)))
        dtt[zh * 16:(zh + 1) * 16, :] = dt
        la = dt * -jnp.exp(cols[:16, 7:8])
        for b in range(2):
            cumt[zh * 16:(zh + 1) * 16, b * SPAN:(b + 1) * SPAN] = exact_dot(la[:, b * SPAN:(b + 1) * SPAN], upper)
    cumc[...] = jnp.concatenate([cumt[...], jnp.zeros((96, T), F32)], axis=0).T
    for i, ref in enumerate((dtt, cumt, cumc, stept, statet, bc, bct, cbt, prm, spar)):
        put(10 + i, ref, small_o[1 + i])

    def put_weights(kind, begin):
        for n in range(8):
            zh, q = n % 2, n // 2
            pltpu.make_async_copy(w.at[zh, q, :, :, :, :, pl.ds(begin, 768)], w_o.at[kind, q, zh], w_sem.at[kind]).start()

    arrived(1)
    put_weights(2, 256)

    @pl.loop(0, 6)
    def _(n):
        zh, c, off, base = group_at(n)
        cols = group_cols(prm, zh, c)
        skip = group_skip(prm, zh, c)
        cc = pltpu.roll(cumc[...], 128 - base, 1)
        ut[pl.ds(off, WIDE), :] = dot(x[...], weight(zh, pl.multiple_of(256 + c * WIDE, WIDE))).T.astype(BF16)
        for i in range(GROUP):
            r = slice(i * HEAD, (i + 1) * HEAD)
            rows = pl.ds(pl.multiple_of(off + i * HEAD, HEAD), HEAD)
            p, _ = conv(ut[rows, :].astype(F32), cols[r])
            sp = sig(p)
            xs = p * sp
            xsb = xs.astype(BF16)
            xst[rows, :] = xsb
            dsil[rows, :] = (sp + xs * (1.0 - sp)).astype(BF16)
            xs = xsb.astype(F32)
            cum = cumt[pl.ds(base + i, 1), :]
            xdt = xs * dtt[pl.ds(base + i, 1), :]
            xdtb = xdt.astype(BF16)
            ys = []
            for b in range(2):
                m = (decay(cum, cc[b * SPAN:(b + 1) * SPAN, i:i + 1], b) * cbt[b]).astype(BF16)
                ys.append(dot(xdtb[:, b * SPAN:(b + 1) * SPAN], m))
            tail = jnp.exp(cum[:, SPAN - 1:SPAN] - cum[:, :SPAN])
            state = dot((xdt[:, :SPAN] * tail).astype(BF16), bc[0:SPAN, 0:128]).astype(BF16)
            ys[1] = ys[1] + jnp.exp(cum[:, SPAN:]) * dot(state, bc[SPAN:, 128:256], 1, 1)
            yt[rows, :] = jnp.concatenate(ys, axis=1) + skip[i:i + 1, 0:1] * xs

        @pl.when(n == 2)
        def _():
            halves(2, 2)
            fulls(2, 3)

    put(3, xst, xst_o)
    put(4, yt, yt_o)
    put(5, ut, ut_o)
    put(9, dsil, dsil_o)
    arrived(2)
    put_weights(1, 1024)

    @pl.loop(0, 6)
    def _(n):
        zh, c, off, _ = group_at(n)
        zt[pl.ds(off, WIDE), :] = dot(x[...], weight(zh, pl.multiple_of(1024 + c * WIDE, WIDE))).T.astype(BF16)
        for i in range(GROUP):
            rows = pl.ds(pl.multiple_of(off + i * HEAD, HEAD), HEAD)
            z = zt[rows, :].astype(F32)
            vb = (yt[rows, :] * (z * sig(z))).astype(BF16)
            vt[rows, :] = vb
            v = vb.astype(F32)
            acc[0, 0:1, :] += jnp.sum(v * v, axis=0, keepdims=True)

        @pl.when(n == 3)
        def _():
            halves(2, 3)

    put(6, zt, zt_o)
    put(7, vt, vt_o)

    c = pltpu.make_async_remote_copy(src_ref=acc.at[0], dst_ref=acc_in.at[0], send_sem=swap_send.at[3], recv_sem=swap_recv.at[3],
                                     device_id=device_at(mate), device_id_type=MESH)
    c.start()
    c.wait()
    sums[0:1, :] = acc[0, 0:1] + acc_in[0, 0:1]

    r_out = lax.rsqrt(sums[0:1, :] / INNER + EPS)

    @pl.loop(0, 6)
    def _(n):
        zh, c, off, _ = group_at(n)
        cols = group_cols(prm, zh, c)
        for i in range(GROUP):
            rows = pl.ds(pl.multiple_of(off + i * HEAD, HEAD), HEAD)
            gat[rows, :] = (vt[rows, :].astype(F32) * r_out * cols[i * HEAD:(i + 1) * HEAD, 5:6]).astype(BF16)
        value = dot(gt[...], gat[pl.ds(off, WIDE), :], 1, 1).astype(BF16)
        pa[zh, :, :, :, :, :, pl.ds(pl.multiple_of(c * WIDE, WIDE), WIDE)] = value.reshape(4, 4, 2, 3, 16, WIDE)

    put(21, gat, gat_o)
    put(22, pa, pa_o)
    arrived(3)
    put_weights(0, 1792)

    @pl.loop(0, 6)
    def _(n):
        zh, c, off, _ = group_at(n)
        cols = group_cols(prm, zh, c)
        dgt[pl.ds(off, WIDE), :] = dot(g[...], weight(zh, pl.multiple_of(1792 + c * WIDE, WIDE))).T.astype(BF16)
        for i in range(GROUP):
            rows = pl.ds(pl.multiple_of(off + i * HEAD, HEAD), HEAD)
            s = dgt[rows, :].astype(F32) * cols[i * HEAD:(i + 1) * HEAD, 5:6] * vt[rows, :].astype(F32)
            acc[1, 0:1, :] += jnp.sum(s, axis=0, keepdims=True)

    put(8, dgt, dgt_o)
    sums[1:2, :] = acc[1, 0:1]
    put(20, sums, small_o[0])
    for piece in range(3):
        for kind in range(4):
            for stage in range(2):
                flight(piece, stage, 0, kind).wait_send()
            for chunk in range(4):
                flight(piece, 2, chunk, kind).wait_send()
    for s in swaps:
        s.wait_send()
    for kind in range(3):
        pltpu.make_async_copy(w_o.at[kind], w_o.at[kind], w_sem.at[kind]).wait()
    for c in out_copies:
        c.wait()


def forward(main, step_w, *others):
    any_ = pl.BlockSpec(memory_space=pl.ANY)
    dma = pltpu.SemaphoreType.DMA
    tall = [sds((1536, T), BF16)] * 9 + [sds((1536, T))]
    big = tall[1:] + [sds((3, 4, 2, 4, 2, 3, 16, 768), BF16), sds((2, 4, 4, 2, 3, 16, 256), BF16), sds((2, 4, 4, 2, 3, 16, 768), BF16)]
    small = [sds((8, T)), sds((32, T)), sds((32, T)), sds((T, 128)), sds((32, T), BF16), sds((256, T), BF16), sds((T, 256), BF16),
             sds((256, T), BF16), sds((2, SPAN, SPAN)), sds((2, 16, 768)), sds((256, 16))]
    return pl.pallas_call(
        forward_kernel, out_shape=big + small, in_specs=[any_] * (2 + len(others)), out_specs=[any_] * 23,
        scratch_shapes=[pltpu.VMEM(a.shape, a.dtype) for a in (step_w, others[2], *others[4:])] + [
                        pltpu.VMEM((2, 4, 4, 2, 3, 16, COLS), BF16), pltpu.VMEM((T, 1536), BF16),
                        pltpu.VMEM((T, 1536), BF16)] + [pltpu.VMEM(s.shape, s.dtype) for s in (*tall, big[-1])] + [
            pltpu.VMEM((2, 8, T), F32), pltpu.VMEM((2, 8, T), F32)] + [pltpu.VMEM(s.shape, s.dtype) for s in small] + [
            dma((6, 3, 4)), dma((6, 3, 4)), dma((25,)), dma((3,)), dma((23,)), dma((4,)), dma((4,))],
        compiler_params=pltpu.CompilerParams(collective_id=0, has_side_effects=True, vmem_limit_bytes=60 << 20),
    )(main, step_w, *others)


SCAN_STEPS = {7: [(0, 2)], 11: [(1, 1)]}
CONV_STEPS = {1: [(0, 3)], 3: [(2, 0)], 5: [(1, 2), (0, 4)]}
TOKEN_STEPS = {0: [(1, 3)], 1: [(2, 1)], 2: [(3, 1), (4, 1)]}


def add_into(target, *others):
    def add(t, o):
        v = t[...].astype(F32)
        for other in o:
            v = v + other[...].astype(F32)
        t[...] = v.astype(BF16)
    if len(target.shape) == 2:
        add(target, others)
    else:
        @pl.loop(0, target.shape[0])
        def _(i):
            add(target.at[i], [o.at[i] for o in others])


def backward_kernel(xt_h, zt_h, ut_h, dgt_h, vt_h, xst_h, dsil_h, gat_h, yt_h, w_h, wst_h, pa_h,
                    *rest_refs):
    small_h, outs_h, scratch = rest_refs[:14], rest_refs[14:19], rest_refs[19:]
    n = len(RCHUNKS)
    part, regions, halves = scratch[0], scratch[1:1 + 9 * n], scratch[1 + 9 * n:1 + 15 * n]
    (xt, xst, zt, dgt, vt, gat, yt, wbuf, wst, total, both, dcbt, ld, dye_all, xe_all, st_all, ds_all, cross, prow, hrow,
     dcum, ddt1, gskip, dstep_t, dbct, dbct_in, dn_in, branch, br_in, dstate, dst, folds,
     sums, dtt, cumt, cumc, stept, statet, bc, bct, cbt, prm, spar, hidden, cot, gain, out, gstate, gsmall, grad_hidden, small, small_in, own_state, ggain, gain_in, quarter, quarters, sums_in,
     send, recv, load_sem, w_sem, swap_send, swap_recv, small_send, small_recv, gain_send, gain_recv, q_send, q_recv, out_sem) = scratch[1 + 15 * n:]
    ut, dyt, dzt, dsil, dut = xst, zt, dgt, vt, zt
    at = place()
    mate = {**at, "core": 1 - at["core"]}
    far = moved(at, "z", 2)
    far_mate = {**far, "core": 1 - at["core"]}
    entered = greet([moved(at, axis, by) for axis in "xyz" for by in (1, 2, 3)] + [mate, far_mate]
                    + [moved(mate, "x", by) for by in (1, 2, 3)])
    mine = pl.ds(pl.multiple_of(at["core"] * 256, 256), 256)
    theirs = pl.ds(pl.multiple_of((1 - at["core"]) * 256, 256), 256)

    loads = [pltpu.make_async_copy(s, d, load_sem.at[i]) for i, (s, d) in enumerate(
        [(vt_h, vt), (yt_h, yt), (zt_h, zt), (dgt_h, dgt), (xt_h, xt), (xst_h, xst), (ut_h, ut), (wst_h, wst), (dsil_h, dsil), (gat_h, gat), (pa_h, part.at[..., pl.ds(0, 768)])]
        + list(zip(small_h, (sums, dtt, cumt, cumc, stept, statet, bc, bct, cbt, prm, spar, hidden, cot, gain))))]
    first = [loads[i] for i in (10, 11, 20, 0, 1, 2, 3, 4)]
    second = [loads[i] for i in (9, 5, 7, *range(12, 20), *range(21, 25))]
    out_copies = []

    def put(i, source):
        c = pltpu.make_async_copy(source, outs_h[i], out_sem.at[i])
        c.start()
        out_copies.append(c)

    def weights(i):
        late = i >= 8
        return pltpu.make_async_copy(w_h.at[jnp.where(late, 0, 1 + i % 2), jnp.where(late, i - 8, i // 2)], wbuf.at[i % 3], w_sem.at[i % 3])

    def product(i, values):
        weights(i).wait()

        @pl.when(i + 2 < 12)
        def _():
            weights(i + 2).start()
        return (dot(wbuf[i % 3, 0].reshape(384, 768), values[0:768, :]) + dot(wbuf[i % 3, 1].reshape(384, 768), values[768:1536, :])).T

    for c in first:
        c.start()
    weights(0).start()
    weights(1).start()
    for c in second:
        c.start()

    def remote(src, dst_ref, s, r, to):
        return pltpu.make_async_remote_copy(src_ref=src, dst_ref=dst_ref, send_sem=s, recv_sem=r, device_id=device_at(to), device_id_type=MESH)

    def block(where, chunk, piece, stage):
        begin, width = RCHUNKS[chunk]
        return part.at[units(where, ORDERS[piece][:2 - stage]) + (piece, slice(None), pl.ds(begin, width))]

    def slot(chunk, piece, stage):
        return (chunk * 3 + piece) * 3 + stage

    def start(chunk, piece, stage, i):
        axis = ORDERS[piece][2 - stage]
        region = regions[slot(chunk, piece, stage)]
        right, left, opposite = moved(at, axis, 1), moved(at, axis, 3), moved(at, axis, 2)
        if (chunk, stage) == (0, 0) and i < 4:
            own = lambda where: pa_h.at[units(where, ORDERS[piece][:2]) + (piece,)]
        else:
            own = lambda where: block(where, chunk, piece, stage)
        if stage == 2:
            to = (right, left, opposite)[i]
            remote(own(to), region.at[i], send.at[chunk, piece, 1], recv.at[chunk, piece, 2, 1], to).start()
            return
        half = halves[(chunk * 3 + piece) * 2 + stage]
        cut = lambda ref, h: half_of(ref, stage, piece, RCHUNKS[chunk][1], h)
        src, dst_ref, to = (
            lambda: (cut(own(opposite), 0), half.at[0], right),
            lambda: (cut(own(opposite), 1), half.at[1], left),
            lambda: (cut(own(right), 1), cut(region.at[0], 1), right),
            lambda: (cut(own(left), 0), cut(region.at[1], 0), left),
            lambda: (cut(own(right), 0), cut(region.at[0], 0), right),
            lambda: (cut(own(left), 1), cut(region.at[1], 1), left))[i]()
        remote(src, dst_ref, send.at[chunk, piece, int(i > 1)], recv.at[chunk, piece, stage, int(i > 1)], to).start()

    def took(buffer, sem):
        pltpu.make_async_copy(buffer, buffer, sem).wait()

    def step(chunk, k):
        stage = k // 2
        for piece in range(3):
            if k % 2:
                half = halves[(chunk * 3 + piece) * 2 + stage]
                took(half, recv.at[chunk, piece, stage, 0])
                axis = ORDERS[piece][2 - stage]
                for h, by in ((0, 1), (1, 3)):
                    mid = block(moved(at, axis, by), chunk, piece, stage)
                    add_into(half_of(mid, stage, piece, RCHUNKS[chunk][1], h), half.at[h])
                    start(chunk, piece, stage, 4 + h)
            else:
                if k > 0:
                    region = regions[slot(chunk, piece, stage - 1)]
                    took(region, recv.at[chunk, piece, stage - 1, 1])
                    add_into(block(at, chunk, piece, stage - 1), *[region.at[i] for i in range(region.shape[0])])
                    if stage < 3:
                        took(halves[(chunk * 3 + piece) * 2 + stage - 1], send.at[chunk, piece, 0])
                    took(region, send.at[chunk, piece, 1])
                if k < 6:
                    for i in range(3 if stage == 2 else 4):
                        start(chunk, piece, stage, i)

    def steps_after(table, index):
        for i, todo in table.items():
            @pl.when(index == i)
            def _(todo=todo):
                for chunk, k in todo:
                    step(chunk, k)

    def gradients(left, right, zh, col):
        for q in range(4):
            value = dot(left[q * 384:(q + 1) * 384, :], right, 1, 1).astype(BF16)
            part[zh, q, :, :, :, :, pl.ds(col, right.shape[0])] = value.reshape(4, 2, 3, 16, right.shape[0])

    def strip(q):
        return pl.ds(pl.multiple_of(q * 384, 128), 384)

    def fold(v):
        return v[:, 0:128] + v[:, 128:256] + v[:, 256:384] + v[:, 384:512]

    def row_sums(v):
        ones = jnp.ones((8, 128), BF16)
        a, b, _ = split(v)
        return (dot(ones, a, 1, 1) + dot(ones, b, 1, 1))[0:1]

    for ref in (dcbt, cross, dcum, ddt1, gskip, ggain):
        ref[...] = jnp.zeros_like(ref)
    first[1].wait()
    entered()
    step(0, 0)
    swap_sums = remote(sums, sums_in, swap_send.at[3], swap_recv.at[3], mate)
    swap_sums.start()
    for c in first[2:]:
        c.wait()
    swap_sums.wait()
    r_out = lax.rsqrt(sums[0:1, :] / INNER + EPS)
    k2 = r_out * r_out * r_out * (sums[1:2, :] + sums_in[1:2, :]) / INNER

    @pl.loop(0, 6)
    def _(m):
        zh, c, off, _ = group_at(m)
        cols = group_cols(prm, zh, c)
        for i in range(GROUP):
            r = slice(i * HEAD, (i + 1) * HEAD)
            rows = pl.ds(pl.multiple_of(off + i * HEAD, HEAD), HEAD)
            z = zt[rows, :].astype(F32)
            dg = dgt[rows, :].astype(F32)
            v = vt[rows, :].astype(F32)
            sz = sig(z)
            zs = z * sz
            dv = dg * cols[r, 5:6] * r_out - v * k2
            folds[0, r, :] = fold(dg * v * r_out)
            dyt[rows, :] = (dv * zs).astype(BF16)
            dzt[rows, :] = (dv * yt[rows, :] * (sz + zs * (1.0 - sz))).astype(BF16)
        prow[zh * 3 + c, 5:6, :] = row_sums(folds[0])
        gradients(xt, dzt[pl.ds(off, WIDE), :], zh, pl.multiple_of(768 + c * WIDE, WIDE))

    first[0].wait()
    step(0, 1)
    step(1, 0)
    loads[8].start()
    for c in second:
        c.wait()

    @pl.loop(0, 6)
    def _(m):
        zh, c, off, base = group_at(m)
        cc = pltpu.roll(cumc[...], 128 - base, 1)
        skips = group_skip(prm, zh, c)
        for i in range(GROUP):
            r = slice(i * HEAD, (i + 1) * HEAD)
            rows = pl.ds(pl.multiple_of(off + i * HEAD, HEAD), HEAD)
            skip = skips[i:i + 1, 0:1]
            xs = xst[rows, :].astype(F32)
            dyb = dyt[rows, :]
            dy = dyb.astype(F32)
            yssm = yt[rows, :] - skip * xs
            gskip[pl.ds(base + i, 1), :] = jnp.sum(dy * xs, axis=0, keepdims=True)
            dt = dtt[pl.ds(base + i, 1), :]
            cum = cumt[pl.ds(base + i, 1), :]
            xdt = xs * dt
            xdtb = xdt.astype(BF16)
            dxs = []
            for b in range(2):
                s = slice(b * SPAN, (b + 1) * SPAN)
                w = decay(cum, cc[s, i:i + 1], b)
                dxs.append(dot(dyb[:, s], (w * cbt[b]).astype(BF16), 1, 1))
                dcbt[b] += dot(xdtb[:, s], dyb[:, s], 0, 0) * w
            tail = jnp.exp(cum[:, SPAN - 1:SPAN] - cum[:, :SPAN])
            xe = (xdt[:, :SPAN] * tail).astype(BF16)
            dye = (dy[:, SPAN:] * jnp.exp(cum[:, SPAN:])).astype(BF16)
            ds = dot(dye, bc[SPAN:, 128:256]).astype(BF16)
            xe_all[r, :] = xe
            dye_all[r, :] = dye
            st_all[r, :] = dot(xe, bc[0:SPAN, 0:128]).astype(BF16)
            ds_all[r, :] = ds
            dxs[0] = dxs[0] + tail * dot(ds, bc[0:SPAN, 0:128], 1, 1)
            dx = jnp.concatenate(dxs, axis=1)
            dcum[pl.ds(base + i, 1), :] = jnp.sum(dy * yssm - xdtb.astype(F32) * dx, axis=0, keepdims=True)
            ddt1[pl.ds(base + i, 1), :] = jnp.sum(xs * dx, axis=0, keepdims=True)
            dyt[rows, :] = (dt * dx + skip * dy).astype(BF16)
            if i % 2:
                steps_after(SCAN_STEPS, m * 2 + i // 2)
        cross[1] += dot(st_all[...], dye_all[...], 0, 0)
        cross[0] += dot(ds_all[...], xe_all[...], 0, 0)

    upper = tri(SPAN, lambda r, c: r <= c).astype(F32)
    for b in range(2):
        s = slice(b * SPAN, (b + 1) * SPAN)
        d = (dcbt[b] * upper).astype(BF16)
        db = dot(bct[128:256, s], d, 1, 1)
        dc = dot(bct[0:128, s], d)
        dbct[0:128, s] = (db + cross[0] if b == 0 else db).astype(BF16)
        dbct[128:256, s] = (dc + cross[1] if b == 1 else dc).astype(BF16)
    swap_bc = remote(dbct, dbct_in, swap_send.at[1], swap_recv.at[1], mate)
    swap_bc.start()
    loads[6].start()

    dla = exact_dot(dcum[...], tri(T, lambda r, c: r >= c))
    for zh in range(2):
        rows = slice(zh * 16, (zh + 1) * 16)
        hc = prm[zh, :, 0:128].T
        rate = -jnp.exp(hc[:16, 7:8])
        d = dla[rows]
        dstep = (ddt1[rows, :] + rate * d) * sig(stept[rows, :].astype(F32) + hc[:16, 6:7])
        gd = jnp.sum(d * dtt[rows, :] * rate, axis=1, keepdims=True)
        hcol = jnp.concatenate([jnp.sum(dstep, axis=1, keepdims=True), gd, jnp.sum(gskip[rows, :], axis=1, keepdims=True),
                                jnp.zeros((16, 125), F32)], axis=1)
        hrow[:, zh * 128:(zh + 1) * 128] = jnp.concatenate([hcol, jnp.zeros((112, 128), F32)], axis=0).T[:8]
        keep = lax.broadcasted_iota(jnp.int32, (16, T), 0) < 12
        dstep_t[zh, 0:16, :] = jnp.where(keep, dstep, 0.0).astype(BF16)
        dstep_t[zh, 16:128, :] = jnp.zeros((112, T), BF16)


    swap_bc.wait_recv()
    for q in range(4):
        r = slice(q * 64, (q + 1) * 64)
        cols = spar[r]
        p, shifted = conv(statet[r, :].astype(F32), cols)
        sp = sig(p)
        dp = (dbct[r, :].astype(F32) + dbct_in[r, :].astype(F32)) * (sp + p * sp * (1.0 - sp))
        dstate[r, :] = conv_back(dp, cols).astype(BF16)
        dst[r, :] = jnp.concatenate([jnp.sum(dp * shifted[k], axis=1, keepdims=True) for k in range(4)]
                                    + [jnp.sum(dp, axis=1, keepdims=True), jnp.zeros((64, 123), F32)], axis=1)
    small[48:56, :] = dst[...].T[:8].astype(BF16)
    for zh in range(2):
        ld[0:64, :] = dstate[pl.ds(zh * 128 + pl.multiple_of(at["core"] * 64, 64), 64), :]
        ld[64:128, :] = dstep_t[zh, 0:64, :]
        gradients(xt, ld[...], zh, STATE_COL)

    step(4, 0)
    loads[6].wait()
    loads[8].wait()

    @pl.loop(0, 6)
    def _(m):
        zh, c, off, _ = group_at(m)
        cols = group_cols(prm, zh, c)
        for i in range(GROUP):
            r = slice(i * HEAD, (i + 1) * HEAD)
            rows = pl.ds(pl.multiple_of(off + i * HEAD, HEAD), HEAD)
            u = ut[rows, :].astype(F32)
            dp = dyt[rows, :].astype(F32) * dsil[rows, :].astype(F32)
            du = cols[r, 0:1] * dp
            folds[0, r, :] = fold(u * dp)
            folds[4, r, :] = fold(dp)
            for k in range(1, 4):
                ahead = sooner(dp, k)
                du = du + cols[r, k:k + 1] * ahead
                folds[k, r, :] = fold(u * ahead)
            dut[rows, :] = du.astype(BF16)
        for k in range(5):
            prow[zh * 3 + c, k:k + 1, :] = row_sums(folds[k])
        gradients(xt, dut[pl.ds(off, WIDE), :], zh, pl.multiple_of(INNER_COL + c * WIDE, 128))
        steps_after(CONV_STEPS, m)

    for q in range(6):
        small[q * 8:(q + 1) * 8, :] = prow[q].astype(BF16)
    small[56:64, :] = hrow[...].astype(BF16)

    def small_flights(s):
        slot_here = small_in.at[s, at["xyz"[s]]]
        return [remote(slot_here, slot_here, small_send.at[s, by - 1], small_recv.at[s, by - 1], moved(at, "xyz"[s], by)) for by in (1, 2, 3)]

    def small_start(s):
        small_in[s, at["xyz"[s]]] = small[...]
        for c in small_flights(s):
            c.start()

    def small_end(s):
        for c in small_flights(s):
            c.wait()
        total4 = small_in[s, 0].astype(F32) + small_in[s, 1].astype(F32) + small_in[s, 2].astype(F32) + small_in[s, 3].astype(F32)
        small[...] = total4.astype(BF16)
        if s == 2:
            gsmall[0:64, :] = total4

    small_start(0)
    step(3, 0)


    @pl.loop(0, 4)
    def _(q):
        more = [dot(wst[zh, q, :, :, :, :, pl.ds(128, 128)].reshape(384, 128), dstep_t[zh]) for zh in range(2)]
        both[...] = product(2 * q, dzt) + product(1 + 2 * q, dut) + (more[0] + more[1]).T
        total[:, strip(q)] = both[mine, :]
        branch[theirs, strip(q)] = both[theirs, :].astype(BF16)
        steps_after(TOKEN_STEPS, q)

    small_end(0)
    small_start(1)
    swap_dn = remote(branch.at[theirs], dn_in, swap_send.at[2], swap_recv.at[2], mate)
    swap_dn.start()
    own_state[...] = dstate[:, mine].T
    step(2, 2)
    swap_dn.wait()

    @pl.loop(0, 2)
    def _(q):
        r = pl.ds(pl.multiple_of(q * 128, 128), 128)
        full = total[r, :] + dn_in[r, :].astype(F32)
        for zh in range(2):
            full = full + dot(own_state[r, zh * 128:(zh + 1) * 128], wst[zh, :, :, :, :, :, pl.ds(0, 128)].reshape(1536, 128), 1, 1)
        h = hidden[r, :].astype(F32)
        r_in = lax.rsqrt(jnp.mean(h * h, axis=1, keepdims=True) + EPS)
        ggain[...] += jnp.sum(full * h * r_in, axis=0, keepdims=True)
        scaled = full * gain[...].reshape(1, 1536)
        back = scaled * r_in - h * (r_in * r_in * r_in * (jnp.sum(scaled * h, axis=1, keepdims=True) / 1536))
        grad_hidden[r, :] = (cot[r, :].astype(F32) + back).astype(BF16)

    def gain_peers(s):
        if s == 0:
            return [moved(at, "x", by) for by in (1, 2, 3)] + [mate] + [moved(mate, "x", by) for by in (1, 2, 3)]
        return [moved(at, "xyz"[s], by) for by in (1, 2, 3)]

    def gain_flights(s):
        here = gain_in.at[s, at["x"] * 2 + at["core"] if s == 0 else at["xyz"[s]]]
        return [remote(here, here, gain_send.at[s, i], gain_recv.at[s, i], to) for i, to in enumerate(gain_peers(s))]

    def gain_start(s, rows):
        gain_in[s, at["x"] * 2 + at["core"] if s == 0 else at["xyz"[s]]] = rows
        for c in gain_flights(s):
            c.start()

    def gain_end(s):
        for c in gain_flights(s):
            c.wait()
        rows = gain_in[s, 0]
        for i in range(1, 8 if s == 0 else 4):
            rows = rows + gain_in[s, i]
        return rows

    gain_start(0, jnp.concatenate([ggain[:, q * 256:(q + 1) * 256] for q in range(6)] + [jnp.zeros((2, 256), F32)], axis=0))
    put(4, grad_hidden)
    step(3, 2)
    step(4, 2)
    step(1, 4)

    def output(first_strip):
        @pl.loop(first_strip, first_strip + 2)
        def _(q):
            branch[:, strip(q)] = product(8 + q, gat).astype(BF16)

    output(0)
    step(2, 3)
    step(3, 3)
    step(4, 3)
    gain_start(1, gain_end(0))
    small_end(1)
    small_start(2)
    output(2)
    swap_br = remote(branch.at[theirs], br_in, swap_send.at[0], swap_recv.at[0], mate)
    swap_br.start()
    step(2, 4)
    step(3, 4)
    step(4, 4)
    gain_start(2, gain_end(1))
    step(1, 6)
    step(0, 6)
    step(4, 6)
    own = units(at, "")
    for piece in range(3):
        quarter[piece * 16:(piece + 1) * 16, :] = part[own + (piece, slice(None), pl.ds(STATE_COL, 128))].astype(F32)
    thirds = [remote(quarter, quarters.at[i], q_send.at[i], q_recv.at[i], to) for i, to in enumerate((mate, far, far_mate))]
    for c in thirds:
        c.start()
    step(2, 6)
    step(3, 6)
    for piece in range(3):
        out[piece * 16:(piece + 1) * 16, :] = part[own + (piece, slice(None), pl.ds(0, 2304))]
    put(0, out)
    swap_br.wait()

    @pl.loop(0, 2)
    def _(q):
        r = pl.ds(pl.multiple_of(q * 128, 128), 128)
        own_rows = pl.ds(pl.multiple_of(at["core"] * 256 + q * 128, 128), 128)
        branch[own_rows, :] = (hidden[r, :].astype(F32) + branch[own_rows, :].astype(F32) + br_in[r, :].astype(F32)).astype(BF16)

    put(3, branch.at[mine])
    small_end(2)
    gsmall[64:72, :] = gain_end(2)
    put(2, gsmall)
    for c in thirds:
        c.wait()
    low = at["core"] == 0
    q0, q1, q2, q3 = quarter[...], quarters[0], quarters[1], quarters[2]
    here = jnp.where(low, jnp.concatenate([q0[:, :64], q1[:, :64]], axis=1), jnp.concatenate([q1[:, :64], q0[:, :64]], axis=1))
    there = jnp.where(low, jnp.concatenate([q2[:, :64], q3[:, :64]], axis=1), jnp.concatenate([q3[:, :64], q2[:, :64]], axis=1))
    first = at["z"] < 2
    gstate[:, 0:128] = jnp.where(first, here, there)
    gstate[:, 128:256] = jnp.where(first, there, here)
    gstate[:, 256:384] = q0
    put(1, gstate)
    swap_bc.wait_send()
    for c in out_copies:
        c.wait()


def backward(tall, small, hidden, cot, gain):
    n = len(RCHUNKS)
    results = [sds((48, 2304), BF16), sds((48, 384)), sds((SUMS + 8, 256)), sds((256, 1536), BF16), sds((256, 1536), BF16)]
    any_ = pl.BlockSpec(memory_space=pl.ANY)
    shapes = [(stage, piece, RCHUNKS[chunk][1]) for chunk in range(n) for piece in range(3) for stage in range(3)]
    regions = [pltpu.VMEM((3 if s[0] == 2 else 2,) + region_shape(*s), BF16) for s in shapes]
    halves = [pltpu.VMEM((2,) + half_shape(*s), BF16) for s in shapes if s[0] < 2]
    dma = pltpu.SemaphoreType.DMA
    v = lambda shape, dtype=F32: pltpu.VMEM(shape, dtype)
    return pl.pallas_call(
        backward_kernel,
        in_specs=[any_] * (len(tall) + len(small) + 3),
        out_specs=[any_] * 5,
        out_shape=results,
        scratch_shapes=[v((2, 4, 4, 2, 3, 16, RCOLS), BF16)] + regions + halves + [
            v((1536, T), BF16)] * 6 + [v((1536, T)), v((3, 2, 4, 2, 3, 16, 768), BF16), v((2, 4, 4, 2, 3, 16, 256), BF16),
            v((256, 1536)), v((T, 384)), v((2, SPAN, SPAN)), v((128, T), BF16), v((WIDE, SPAN), BF16), v((WIDE, SPAN), BF16),
            v((WIDE, 128), BF16), v((WIDE, 128), BF16), v((2, 128, SPAN)), v((6, 8, WIDE)), v((8, 256)),
            v((32, T)), v((32, T)), v((32, T)), v((2, 128, T), BF16), v((256, T), BF16), v((256, T), BF16),
            v((256, 1536), BF16), v((T, 1536), BF16), v((256, 1536), BF16),
            v((256, T), BF16), v((256, 128)), v((5, WIDE, 128))] + [v(a.shape, a.dtype) for a in (*small, hidden, cot, gain, *results[:3], results[4])] + [ v((SUMS, 256), BF16), v((3, 4, SUMS, 256), BF16), v((256, 256), BF16), v((1, 1536)), v((3, 8, 8, 256)), v((48, 128)), v((3, 48, 128)), v((8, T)),
            dma((n, 3, 2)), dma((n, 3, 3, 2)), dma((25,)), dma((3,)), dma((4,)), dma((4,)), dma((3, 3)), dma((3, 3)), dma((3, 7)), dma((3, 7)), dma((3,)), dma((3,)), dma((5,))],
        compiler_params=pltpu.CompilerParams(collective_id=1, has_side_effects=True, vmem_limit_bytes=65400 << 10),
    )(*tall, *small, hidden, cot, gain)


def finish_kernel(out, gstate, small, new_h, grad_h, new_hidden, grad_hidden, in_gain, main, step, state, inner, inner_bias, cstate, cstate_bias,
                  bias, log, skip, out_gain, proj_out):
    new_hidden[...] = new_h[...]
    grad_hidden[...] = grad_h[...]
    z_hi = lax.axis_index("tensor") // 2
    proj_out[...] = out[:, 0:768].astype(F32)
    main[:, 0, :] = out[:, 768:1536].astype(F32)
    main[:, 1, :] = out[:, 1536:2304].astype(F32)
    step[...] = gstate[:, 256:384].T[64:76]
    state[...] = gstate[:, 0:256]
    for c in range(3):
        rows = small[pl.ds(pl.multiple_of(z_hi * 24 + c * 8, 8), 8), :]
        cols = slice(c * 256, (c + 1) * 256)
        inner[:, cols] = rows[0:4]
        inner_bias[cols] = rows[4:5].reshape(256)
        out_gain[cols] = rows[5:6].reshape(256)
    cstate[...] = small[48:52, :]
    cstate_bias[...] = small[52:53, :].reshape(256)
    for q in range(6):
        in_gain[q * 256:(q + 1) * 256] = small[64 + q:65 + q, :].reshape(256)
    heads = small[56:64, pl.ds(pl.multiple_of(z_hi * 128, 128), 128)]
    for i, ref in enumerate((bias, log, skip)):
        ref[...] = heads[i:i + 1, 0:12].reshape(12)


def finish(out, gstate, small, new_hidden, grad_hidden):
    vm = pl.BlockSpec(memory_space=pltpu.VMEM)
    shapes = [sds(s) for s in ((1536,), (48, 2, 768), (12, 48), (48, 256), (4, 768), (768,), (4, 256), (256,), (12,), (12,), (12,), (768,), (48, 768))]
    return pl.pallas_call(
        finish_kernel, out_shape=[sds((256, 1536), BF16)] * 2 + shapes, in_specs=[vm] * 5, out_specs=[vm] * 15,
    )(out, gstate, small, new_hidden, grad_hidden)


def per_device(hidden, in_gain, proj_main, proj_step, proj_state, conv_inner, conv_inner_bias, conv_state, conv_state_bias,
               step_bias, decay_log, skip_gain, out_gain, proj_out, grad_out):
    outs = forward(proj_main.reshape(48, 1536), proj_step.T, proj_state, proj_out, hidden, grad_out, conv_inner, conv_state,
                   conv_inner_bias, out_gain, conv_state_bias, in_gain, step_bias, decay_log, skip_gain)
    results = backward(outs[:12], outs[12:], hidden, grad_out, in_gain)
    new_hidden, grad_hidden, ggain, main, step, *others = finish(*results)
    return (new_hidden, grad_hidden, ggain, main, step.T, *others)


def solution(mesh):
    rows = P(("dp", "tensor"), None)
    per_head = P("tensor")
    in_specs = (rows, P(), P("dp", None, "tensor"), P("dp", "tensor"), P("dp", None), P(None, "tensor"), per_head, P(), P(),
                per_head, per_head, per_head, per_head, P("dp", "tensor"), rows)
    out_specs = (rows, rows, P(), P("dp", None, "tensor"), P("dp", "tensor"), P("dp", None), P(None, "tensor"), per_head, P(), P(),
                 per_head, per_head, per_head, per_head, P("dp", "tensor"))
    return jax.shard_map(per_device, mesh=mesh, in_specs=in_specs, out_specs=out_specs, check_vma=False)
```

profile of v0, /device:TPU:1, one launch (start us, length us, event | category | flops | bytes accessed | tf_op | source)
XLA Modules:
  0.0 165.1 jit_solution(15428156402665479071)
XLA Ops:
  0.6 1.6 copy.30
  2.2 83.6 %shard_map.262 = (bf16[1536,512]{1,0:T(8,128)(2,1)}, bf16[1536,512]{1,0:T(8,128)(2,1)}, bf16[1536,512]{1,0:T(8,128)(2,1)}, bf16[1536,512]{1,0:T(8,128)(2,1)}, bf...) custom-call(bf16[48,1536]{1,0:T(8,128)(2,1)} %bitcast.4, ...), custom_call_target="tpu_custom_call" | custom-call | tf_op jit(solution)/shard_map/pallas_call | solution.py:412
  85.8 76.2 %shard_map.263 = (bf16[48,2304]{1,0:T(8,128)(2,1)}, f32[48,384]{1,0:T(8,128)}, f32[72,256]{1,0:T(8,128)}, bf16[256,1536]{1,0:T(8,128)(2,1)}, bf16[256,1536]{1,0:T(8,128)(2,1)}) custom-call(bf16[1536,512]{1,0:T(8,128)(2,1)} %get-tuple-element.58.xt_h, bf16[1536,512]{1,0:T(8,128)(2,1)} %get-tuple-element.59.zt_h, bf16[1536,512]{1,0:T(8,128)(2,1)} %get-tuple-element.60.ut_h, ...), custom_call_target="tpu_custom_call" | custom-call | tf_op jit(solution)/shard_map/pallas_call | solution.py:877
  162.1 2.9 %shard_map.264 = (bf16[256,1536]{1,0:T(8,128)(2,1)}, bf16[256,1536]{1,0:T(8,128)(2,1)}, f32[1536]{0:T(1024)}, f32[48,2,768]{2,1,0:T(2,128)}, f32[12,48]{1,0:T(8,...) custom-call(bf16[48,2304]{1,0:T(8,128)(2,1)} %get-tuple-element.81.o, ...), custom_call_target="tpu_custom_call" | custom-call | tf_op jit(solution)/shard_map/pallas_call | solution.py:922
where the time goes:
time: 165 us
  Pallas kernels  163 us (99%)
    pallas_call x1, Pallas kernels, forward(): pl.pallas_call(forward_kernel, out_shape=big + small, in_specs=[any_] * (...  83.6 us
    pallas_call x1, Pallas kernels, backward(): pl.pallas_call(backward_kernel, in_specs=[any_] * (len(tall) + len(small)...  76.2 us

commit v1 on v0

--- a/solution.py
+++ b/solution.py
@@ -454,7 +454,8 @@
     far = moved(at, "z", 2)
     far_mate = {**far, "core": 1 - at["core"]}
     entered = greet([moved(at, axis, by) for axis in "xyz" for by in (1, 2, 3)] + [mate, far_mate]
-                    + [moved(mate, "x", by) for by in (1, 2, 3)])
+                    + [moved(mate, "x", by) for by in (1, 2, 3)]
+                    + [moved(moved(at, "y", a), "z", b) for a in (1, 2, 3) for b in (1, 2, 3)])
     mine = pl.ds(pl.multiple_of(at["core"] * 256, 256), 256)
     theirs = pl.ds(pl.multiple_of((1 - at["core"]) * 256, 256), 256)
 
@@ -755,12 +756,12 @@
         branch[theirs, strip(q)] = both[theirs, :].astype(BF16)
         steps_after(TOKEN_STEPS, q)
 
-    small_end(0)
-    small_start(1)
     swap_dn = remote(branch.at[theirs], dn_in, swap_send.at[2], swap_recv.at[2], mate)
     swap_dn.start()
     own_state[...] = dstate[:, mine].T
     step(2, 2)
+    small_end(0)
+    small_start(1)
     swap_dn.wait()
 
     @pl.loop(0, 2)
@@ -779,14 +780,17 @@
     def gain_peers(s):
         if s == 0:
             return [moved(at, "x", by) for by in (1, 2, 3)] + [mate] + [moved(mate, "x", by) for by in (1, 2, 3)]
-        return [moved(at, "xyz"[s], by) for by in (1, 2, 3)]
+        return [moved(moved(at, "y", a), "z", b) for a in range(4) for b in range(4) if a or b]
+
+    def gain_slot(s):
+        return at["x"] * 2 + at["core"] if s == 0 else at["y"] * 4 + at["z"]
 
     def gain_flights(s):
-        here = gain_in.at[s, at["x"] * 2 + at["core"] if s == 0 else at["xyz"[s]]]
+        here = gain_in.at[s, gain_slot(s)]
         return [remote(here, here, gain_send.at[s, i], gain_recv.at[s, i], to) for i, to in enumerate(gain_peers(s))]
 
     def gain_start(s, rows):
-        gain_in[s, at["x"] * 2 + at["core"] if s == 0 else at["xyz"[s]]] = rows
+        gain_in[s, gain_slot(s)] = rows
         for c in gain_flights(s):
             c.start()
 
@@ -794,7 +798,7 @@
         for c in gain_flights(s):
             c.wait()
         rows = gain_in[s, 0]
-        for i in range(1, 8 if s == 0 else 4):
+        for i in range(1, 8 if s == 0 else 16):
             rows = rows + gain_in[s, i]
         return rows
 
@@ -822,7 +826,6 @@
     step(2, 4)
     step(3, 4)
     step(4, 4)
-    gain_start(2, gain_end(1))
     step(1, 6)
     step(0, 6)
     step(4, 6)
@@ -847,7 +850,7 @@
 
     put(3, branch.at[mine])
     small_end(2)
-    gsmall[64:72, :] = gain_end(2)
+    gsmall[64:72, :] = gain_end(1)
     put(2, gsmall)
     for c in thirds:
         c.wait()
@@ -885,8 +888,8 @@
             v((WIDE, 128), BF16), v((WIDE, 128), BF16), v((2, 128, SPAN)), v((6, 8, WIDE)), v((8, 256)),
             v((32, T)), v((32, T)), v((32, T)), v((2, 128, T), BF16), v((256, T), BF16), v((256, T), BF16),
             v((256, 1536), BF16), v((T, 1536), BF16), v((256, 1536), BF16),
-            v((256, T), BF16), v((256, 128)), v((5, WIDE, 128))] + [v(a.shape, a.dtype) for a in (*small, hidden, cot, gain, *results[:3], results[4])] + [ v((SUMS, 256), BF16), v((3, 4, SUMS, 256), BF16), v((256, 256), BF16), v((1, 1536)), v((3, 8, 8, 256)), v((48, 128)), v((3, 48, 128)), v((8, T)),
-            dma((n, 3, 2)), dma((n, 3, 3, 2)), dma((25,)), dma((3,)), dma((4,)), dma((4,)), dma((3, 3)), dma((3, 3)), dma((3, 7)), dma((3, 7)), dma((3,)), dma((3,)), dma((5,))],
+            v((256, T), BF16), v((256, 128)), v((5, WIDE, 128))] + [v(a.shape, a.dtype) for a in (*small, hidden, cot, gain, *results[:3], results[4])] + [ v((SUMS, 256), BF16), v((3, 4, SUMS, 256), BF16), v((256, 256), BF16), v((1, 1536)), v((2, 16, 8, 256)), v((48, 128)), v((3, 48, 128)), v((8, T)),
+            dma((n, 3, 2)), dma((n, 3, 3, 2)), dma((25,)), dma((3,)), dma((4,)), dma((4,)), dma((3, 3)), dma((3, 3)), dma((2, 15)), dma((2, 15)), dma((3,)), dma((3,)), dma((5,))],
         compiler_params=pltpu.CompilerParams(collective_id=1, has_side_effects=True, vmem_limit_bytes=65400 << 10),
     )(*tall, *small, hidden, cot, gain)
 

time: 165 us -> 166 us (level)
  no operation moved by 1% of the time
where the time goes in v1:
time: 166 us; the launch traced here: 165 us
  Pallas kernels  163 us (98%)
    pallas_call x1, Pallas kernels, forward(): pl.pallas_call(forward_kernel, out_shape=big + small, in_specs=[any_] * (...  83.6 us
    pallas_call x1, Pallas kernels, backward(): pl.pallas_call(backward_kernel, in_specs=[any_] * (len(tall) + len(small)...  76.6 us

profile of v1, /device:TPU:1, one launch (start us, length us, event | category | flops | bytes accessed | tf_op | source)
XLA Modules:
  0.0 165.4 jit_solution(10937069667111759177)
XLA Ops:
  0.6 1.6 copy.30
  2.2 83.6 %shard_map.262 = (bf16[1536,512]{1,0:T(8,128)(2,1)}, bf16[1536,512]{1,0:T(8,128)(2,1)}, bf16[1536,512]{1,0:T(8,128)(2,1)}, bf16[1536,512]{1,0:T(8,128)(2,1)}, bf...) custom-call(bf16[48,1536]{1,0:T(8,128)(2,1)} %bitcast.4, ...), custom_call_target="tpu_custom_call" | custom-call | tf_op jit(solution)/shard_map/pallas_call | solution.py:412
  85.8 76.6 %shard_map.263 = (bf16[48,2304]{1,0:T(8,128)(2,1)}, f32[48,384]{1,0:T(8,128)}, f32[72,256]{1,0:T(8,128)}, bf16[256,1536]{1,0:T(8,128)(2,1)}, bf16[256,1536]{1,0:T(8,128)(2,1)}) custom-call(bf16[1536,512]{1,0:T(8,128)(2,1)} %get-tuple-element.58.xt_h, bf16[1536,512]{1,0:T(8,128)(2,1)} %get-tuple-element.59.zt_h, bf16[1536,512]{1,0:T(8,128)(2,1)} %get-tuple-element.60.ut_h, ...), custom_call_target="tpu_custom_call" | custom-call | tf_op jit(solution)/shard_map/pallas_call | solution.py:880
  162.4 2.9 %shard_map.264 = (bf16[256,1536]{1,0:T(8,128)(2,1)}, bf16[256,1536]{1,0:T(8,128)(2,1)}, f32[1536]{0:T(1024)}, f32[48,2,768]{2,1,0:T(2,128)}, f32[12,48]{1,0:T(8,...) custom-call(bf16[48,2304]{1,0:T(8,128)(2,1)} %get-tuple-element.81.o, ...), custom_call_target="tpu_custom_call" | custom-call | tf_op jit(solution)/shard_map/pallas_call | solution.py:925
